TPU v7x, 32 devices: a whole 2x2x4 slice. The times are simulated.
32 devices in a mesh: seed: 2 (over x), tm: 16 (over z, y, core).
Axes of the slice: x: 2, y: 2, z: 4, core: 2. Of those that a mesh axis runs over, the one named last changes fastest.
Arguments:
- queries: bfloat16 [8192, 2560], P(('seed', 'tm')), parts along dimension 0, may hold values from -8 to 8
- keys: bfloat16 [8192, 2560], P(('seed', 'tm')), parts along dimension 0, may hold values from -6 to 6
- values: bfloat16 [8192, 2560], P(('seed', 'tm')), parts along dimension 0, may hold values from -6 to 6
- far_pick: int32 [32, 3], P('tm'), may hold values from 0 to 3
Outputs:
- attended: bfloat16 [8192, 2560], P(('seed', 'tm')), parts along dimension 0
There are 2 independent parts, one for each index of `seed`. A program takes and returns all parts, laid end to end along the dimension named above; an argument that names none is the same for every part. Nothing has to cross between parts.
All inputs are finite; a program needn't handle non-finite values.
Results may differ from a plain program's by a relative error of at most 0.0034.
Values may be sent and summed in bfloat16 or wider, within the bound.
A program may use at most 64 MiB of HBM per device.

v0:
```python
import math

import jax
import jax.numpy as jnp
from jax import lax
from jax.sharding import PartitionSpec as P

H = 20
HD = 128
FAR_ROWS = 64


FAR_SHIFTS = (2, -4, 8)


def extended(array, sides, width):
    for axis, dim in sides:
        size, length = (lax.axis_size(axis), array.shape[dim])
        up = [(i, (i + 1) % size) for i in range(size - 1)]
        down = [(j, i) for i, j in up]
        last = lax.slice_in_dim(array, length - width, length, axis=dim)
        initial = lax.slice_in_dim(array, 0, width, axis=dim)
        before = lax.ppermute(last, axis, up)
        after = lax.ppermute(initial, axis, down)
        array = jnp.concatenate([before, array, after], axis=dim)
    return array


def shifted(value, axis, steps):
    count = lax.axis_size(axis)
    initial, last = (max(0, -steps), min(count, count - steps))
    return lax.ppermute(value, axis, [(source, source + steps) for source in range(initial, last)])


def attend(query_tile, key_tile, value_tile, usable):
    row_count = query_tile.shape[0]
    query_heads = query_tile.reshape(row_count, H, HD)
    key_heads = key_tile.reshape(-1, H, HD)
    value_heads = value_tile.reshape(-1, H, HD)
    scores = jnp.einsum(
        "qhd,khd->hqk", query_heads, key_heads, preferred_element_type=jnp.float32
    ) * (1.0 / math.sqrt(HD))
    scores = jnp.where(usable[None, None, :], scores, -jnp.inf)
    maxima = jnp.max(scores, axis=2, keepdims=True)
    weights = jnp.exp(scores - maxima)
    totals = jnp.sum(weights, axis=2)
    mixed = jnp.einsum(
        "hqk,khd->qhd",
        weights.astype(jnp.bfloat16),
        value_heads,
        preferred_element_type=jnp.float32,
    )
    return (
        (mixed / jnp.transpose(totals)[:, :, None]).reshape(row_count, H * HD).astype(jnp.bfloat16)
    )


def on_device(queries, keys, values, far_pick):
    row_count, feature_width = queries.shape
    tile_count = far_pick.shape[0]
    tile_rows = row_count // tile_count
    device_count = lax.axis_size("tm")
    my_index = lax.axis_index("tm")
    stacked = jnp.stack([keys, values], 0)
    tiled_pair = stacked.reshape(2, tile_count, tile_rows, feature_width)
    framed = extended(tiled_pair, (("tm", 1),), 1)
    piece_count = row_count // FAR_ROWS
    far_members = []
    far_flags = []
    for cycle_index, offset in enumerate(FAR_SHIFTS):
        wanted = far_pick[:, cycle_index]
        arrived = shifted(stacked, "tm", offset)
        chosen = arrived.reshape(2, piece_count, FAR_ROWS, feature_width)[:, wanted]
        source = my_index - offset
        far_members.append(chosen)
        far_flags.append((source >= 0) & (source < device_count))
    far_usable = jnp.repeat(jnp.stack(far_flags), FAR_ROWS)
    outputs = []
    for tile_index in range(tile_count):
        near_pair = framed[:, tile_index : tile_index + 3].reshape(2, 3 * tile_rows, feature_width)
        far_pair = jnp.concatenate([member[:, tile_index] for member in far_members], axis=1)
        global_tile = (
            my_index * tile_count
            + tile_index
            - 1
            + jnp.arange(3 * tile_rows, dtype=jnp.int32) // tile_rows
        )
        near_usable = (global_tile >= 0) & (global_tile < device_count * tile_count)
        usable = jnp.concatenate([near_usable, far_usable], 0)
        key_tile = jnp.concatenate([near_pair[0], far_pair[0]], 0)
        value_tile = jnp.concatenate([near_pair[1], far_pair[1]], 0)
        query_tile = queries[tile_index * tile_rows : (tile_index + 1) * tile_rows]
        outputs.append(attend(query_tile, key_tile, value_tile, usable))
    return jnp.concatenate(outputs, 0)


def solution(mesh):
    return jax.shard_map(
        on_device,
        mesh=mesh,
        in_specs=(
            P(("seed", "tm"), None),
            P(("seed", "tm"), None),
            P(("seed", "tm"), None),
            P("tm", None),
        ),
        out_specs=P(("seed", "tm"), None),
        check_vma=False,
    )
```

profile of v0, /device:TPU:16, one launch (start us, length us, event | category | flops | bytes accessed | tf_op | source)
XLA Modules:
  0.0 254.4 jit_solution(9820988855359657878)
XLA Ops:
  0.0 3.6 %pad_maximum_fusion.1 = bf16[2,256,2560]{2,1,0:T(8,128)(2,1)} fusion(bf16[1,256,2560]{2,1,0:T(8,128)(2,1)} %bitcast.77, bf16[1,256,2560]{2,1,0:T(8,128)(2,1)} %bitcast.80), kind=kLoop, calls=%fused_computation.43 | loop fusion | flops 1310720 | bytes 5242880 | tf_op jit(solution)/shard_map/stack | solution.py:64
  3.6 3.4 %collective-permute-start.1 = (bf16[2,256,2560]{2,1,0:T(8,128)(2,1)}, bf16[2,256,2560]{2,1,0:T(8,128)(2,1)}, u32[]{:S(2)}, u32[]{:S(2)}) collective-permute-start(bf16[2,256,2560]{2,1,0:T(8,128)(2,1)} %pad_maximum_fusion.1), channel_id=1, source_target_pairs={{0,2},{1,3},{2,4},{3,5},{4,6},{5,7},{6,8},{7,9},{8,10},{9,11},{10,... | collective-permute-start | bytes 7864328 | tf_op jit(solution)/shard_map/ppermute | solution.py:32
  7.1 2.4 collective-permute-start.2
  9.4 1.3 collective-permute-start.3
  10.8 1.7 fusion.42
  12.5 1.9 collective-permute-start
  14.4 8.1 %collective-permute-start.4 = (bf16[2,1,128,2560]{3,2,1,0:T(8,128)(2,1)}, bf16[2,1,128,2560]{3,2,1,0:T(8,128)(2,1)}, u32[]{:S(2)}, u32[]{:S(2)}) collective-permute-start(bf16[2,1,128,2560]{3,2,1,0:T(8,128)(2,1)} %get-tuple-element.15), channel_id=1, source_target_pairs={{1,0},{2,1},{3,2},{4,3},{5,4},{6,5},{7,6},{8,7},{9,8},{10,9},{11,1... | collective-permute-start | bytes 3932168 | tf_op jit(solution)/shard_map/ppermute | solution.py:24
  22.5 1.0 fusion.71
  23.7 2.2 copy.23
  25.9 1.1 copy.24
  27.2 164.6 %collective-permute-done = bf16[2,1,128,2560]{3,2,1,0:T(8,128)(2,1)} collective-permute-done((bf16[2,1,128,2560]{3,2,1,0:T(8,128)(2,1)}, bf16[2,1,128,2560]{3,2,1,0:T(8,128)(2,1)}, u32[]{:S(2)}, u32[]{:S(2)}) %collective-permute-start) | collective-permute-done | bytes 1310752 | tf_op jit(solution)/shard_map/ppermute | solution.py:23
  191.8 2.2 maximum_maximum_fusion
  193.9 3.4 %fusion.67 = (bf16[1,3,128,2560]{3,2,1,0:T(8,128)(2,1)}, bf16[1,3,128,2560]{3,2,1,0:T(8,128)(2,1)}, bf16[1,3,128,2560]{3,2,1,0:T(8,128)(2,1)}, bf16[1,3,128,2560]{3,2,1,0:T(8,128)(2,1)}) fusion(bf16[2,3,128,2560]{3,2,1,0:T(8,128)(2,1)S(1)} %get-tuple-element.12, bf16[2,3,128,2560]{3,2,1,0:T(8,128)(2,1)S(1)} %get-tuple-element.13), kind=kLoop, calls=%fused_computation.90 | loop fusion | bytes 15728640 | tf_op jit(solution)/shard_map/slice | solution.py:91
  197.4 3.0 %concatenate.61 = bf16[384,20,128]{2,1,0:T(8,128)(2,1)S(1)} reshape(bf16[1,3,128,2560]{3,2,1,0:T(8,128)(2,1)} %get-tuple-element.9) | data formatting | bytes 3932160 | tf_op jit(solution)/shard_map/concatenate | solution.py:90
  200.4 1.7 copy.9
  202.1 3.0 %concatenate.56 = bf16[384,20,128]{2,1,0:T(8,128)(2,1)S(1)} reshape(bf16[1,3,128,2560]{3,2,1,0:T(8,128)(2,1)} %get-tuple-element.8) | data formatting | bytes 3932160 | tf_op jit(solution)/shard_map/concatenate | solution.py:91
  205.1 1.7 copy.7
  206.8 3.0 %concatenate.70 = bf16[384,20,128]{2,1,0:T(8,128)(2,1)S(1)} reshape(bf16[1,3,128,2560]{3,2,1,0:T(8,128)(2,1)} %get-tuple-element.34) | data formatting | bytes 3932160 | tf_op jit(solution)/shard_map/concatenate | solution.py:90
  209.9 1.7 copy.15
  211.6 3.0 %concatenate.65 = bf16[384,20,128]{2,1,0:T(8,128)(2,1)S(1)} reshape(bf16[1,3,128,2560]{3,2,1,0:T(8,128)(2,1)} %get-tuple-element.35) | data formatting | bytes 3932160 | tf_op jit(solution)/shard_map/concatenate | solution.py:91
  214.6 1.7 copy.13
  216.3 2.4 gather_fusion
  218.7 2.4 gather_fusion.1
  221.1 1.0 slice_bitcast_fusion.5
  222.1 1.2 slice_bitcast_fusion.4
  223.2 2.4 gather_fusion.2
  225.8 1.0 copy-done.4
  227.0 0.3 pad_maximum_fusion.2
  227.3 1.4 fusion.69
  228.7 1.7 concatenate.62
  230.3 1.2 copy.10
  231.5 1.7 concatenate.58
  233.2 0.2 copy.8
  233.4 2.9 %bitcast_reduce_fusion.1 = (f32[20,128]{1,0:T(8,128)S(1)}, f32[20,576,128]{2,1,0:T(8,128)S(1)}) fusion(pred[576]{0:T(1024)(128)(4,1)S(1)} %get-tuple-element.28, bf16[128,20,128]{0,2,1:T(8,128)(2,1)} %bitcast.87, bf16[192,20,128]{2,0,1:T(8,128)(2,1)} %copy.10, bf16[384,20,128]{2,0,1:T(8,128)(2,1)} %copy.9), kind=kOutput, calls=%fused_computation.7 | convolution fusion | flops 387806720 | bytes 9513536 | tf_op jit(solution)/shard_map/qhd,khd->hqk/dot_general | solution.py:40
  236.3 1.3 fusion.2
  237.6 0.3 copy-done.7
  237.9 2.4 divide_convert_fusion.1
  240.2 1.1 copy.19
  241.3 1.1 fusion.70
  242.4 1.7 concatenate.71
  244.1 1.2 copy.16
  245.2 0.8 concatenate.67
  246.3 2.8 %bitcast_reduce_fusion = (f32[20,128]{1,0:T(8,128)S(1)}, f32[20,576,128]{2,1,0:T(8,128)S(1)}) fusion(pred[576]{0:T(1024)(128)(4,1)S(1)} %get-tuple-element.29, bf16[128,20,128]{0,2,1:T(8,128)(2,1)S(1)} %bitcast.86, bf16[192,20,128]{2,0,1:T(8,128)(2,1)} %copy.16, bf16[384,20,128]{2,0,1:T(8,128)(2,1)} %copy.15), kind=kOutput, calls=%fused_computation.4 | convolution fusion | flops 387806720 | bytes 9513536 | tf_op jit(solution)/shard_map/qhd,khd->hqk/dot_general | solution.py:40
  249.1 1.3 fusion.4
  250.5 0.2 copy-done.6
  250.7 2.4 divide_convert_fusion
  253.0 0.2 copy.20
  253.3 1.1 pad_maximum_fusion.5
  (34 shorter events, 1.1 us)
Async XLA Ops:
  0.0 10.7 %copy-start = (bf16[256,2560]{1,0:T(8,128)(2,1)S(1)}, bf16[256,2560]{1,0:T(8,128)(2,1)}, u32[]{:S(2)}) copy-start(bf16[256,2560]{1,0:T(8,128)(2,1)} %param.6) | copy-start | bytes 3932164
  0.0 10.7 %copy-start.1 = (bf16[256,2560]{1,0:T(8,128)(2,1)S(1)}, bf16[256,2560]{1,0:T(8,128)(2,1)}, u32[]{:S(2)}) copy-start(bf16[256,2560]{1,0:T(8,128)(2,1)} %param.5) | copy-start | bytes 3932164
  3.6 212.7 %collective-permute-start.1 = (bf16[2,256,2560]{2,1,0:T(8,128)(2,1)}, bf16[2,256,2560]{2,1,0:T(8,128)(2,1)}, u32[]{:S(2)}, u32[]{:S(2)}) collective-permute-start(bf16[2,256,2560]{2,1,0:T(8,128)(2,1)} %pad_maximum_fusion.1), channel_id=1, source_target_pairs={{0,2},{1,3},{2,4},{3,5},{4,6},{5,7},{6,8},{7,9},{8,10},{9,11},{10,... | collective-permute-start | bytes 7864328 | tf_op jit(solution)/shard_map/ppermute | solution.py:32
  7.1 211.7 %collective-permute-start.2 = (bf16[2,256,2560]{2,1,0:T(8,128)(2,1)}, bf16[2,256,2560]{2,1,0:T(8,128)(2,1)}, u32[]{:S(2)}, u32[]{:S(2)}) collective-permute-start(bf16[2,256,2560]{2,1,0:T(8,128)(2,1)} %pad_maximum_fusion.1), channel_id=1, source_target_pairs={{4,0},{5,1},{6,2},{7,3},{8,4},{9,5},{10,6},{11,7},{12,8},{13,9},{1... | collective-permute-start | bytes 7864328 | tf_op jit(solution)/shard_map/ppermute | solution.py:32
  9.4 213.8 %collective-permute-start.3 = (bf16[2,256,2560]{2,1,0:T(8,128)(2,1)}, bf16[2,256,2560]{2,1,0:T(8,128)(2,1)}, u32[]{:S(2)}, u32[]{:S(2)}) collective-permute-start(bf16[2,256,2560]{2,1,0:T(8,128)(2,1)} %pad_maximum_fusion.1), channel_id=1, source_target_pairs={{0,8},{1,9},{2,10},{3,11},{4,12},{5,13},{6,14},{7,15},{16,24},{17,... | collective-permute-start | bytes 7864328 | tf_op jit(solution)/shard_map/ppermute | solution.py:32
  10.7 11.8 %copy-start.8 = (bf16[256,2560]{1,0:T(8,128)(2,1)S(1)}, bf16[256,2560]{1,0:T(8,128)(2,1)}, u32[]{:S(2)}) copy-start(bf16[256,2560]{1,0:T(8,128)(2,1)} %param.4) | copy-start | bytes 3932164
  12.5 179.3 %collective-permute-start = (bf16[2,1,128,2560]{3,2,1,0:T(8,128)(2,1)}, bf16[2,1,128,2560]{3,2,1,0:T(8,128)(2,1)}, u32[]{:S(2)}, u32[]{:S(2)}) collective-permute-start(bf16[2,1,128,2560]{3,2,1,0:T(8,128)(2,1)} %get-tuple-element.14), channel_id=1, source_target_pairs={{0,1},{1,2},{2,3},{3,4},{4,5},{5,6},{6,7},{7,8},{8,9},{9,10},{10,1... | collective-permute-start | bytes 3932168 | tf_op jit(solution)/shard_map/ppermute | solution.py:23
  14.4 12.6 %copy-start.10 = (s32[2,3]{1,0:T(2,128)S(1)}, s32[2,3]{1,0:T(2,128)}, u32[]{:S(2)}) copy-start(s32[2,3]{1,0:T(2,128)} %param.7) | copy-start | bytes 76
  14.4 177.3 %collective-permute-start.4 = (bf16[2,1,128,2560]{3,2,1,0:T(8,128)(2,1)}, bf16[2,1,128,2560]{3,2,1,0:T(8,128)(2,1)}, u32[]{:S(2)}, u32[]{:S(2)}) collective-permute-start(bf16[2,1,128,2560]{3,2,1,0:T(8,128)(2,1)} %get-tuple-element.15), channel_id=1, source_target_pairs={{1,0},{2,1},{3,2},{4,3},{5,4},{6,5},{7,6},{8,7},{9,8},{10,9},{11,1... | collective-permute-start | bytes 3932168 | tf_op jit(solution)/shard_map/ppermute | solution.py:24
  223.2 2.6 %copy-start.3 = (bf16[2,64,2560]{2,1,0:T(8,128)(2,1)S(1)}, bf16[2,64,2560]{2,1,0:T(8,128)(2,1)}, u32[]{:S(2)}) copy-start(bf16[2,64,2560]{2,1,0:T(8,128)(2,1)} %get-tuple-element.21) | copy-start | bytes 1966084
  225.7 1.1 copy-start.4
  225.7 1.3 copy-start.5
  236.3 1.5 copy-start.7
  245.2 1.1 copy-start.9
  249.1 1.5 copy-start.6
  250.7 2.6 %copy-start.2 = (bf16[128,2560]{1,0:T(8,128)(2,1)S(1)}, bf16[128,2560]{1,0:T(8,128)(2,1)}, u32[]{:S(2)}) copy-start(bf16[128,2560]{1,0:T(8,128)(2,1)} %copy.19) | copy-start | bytes 1966084
where the time goes:
time: 255 us; the launch traced here: 254 us
  waiting for transfers between devices  165 us (65%)
  local copies, waits for them, and re-layouts  50.2 us (20%)
  starting transfers between devices  17.1 us (7%)
  other arithmetic  11.8 us (5%)
  matrix products  10.4 us (4%)
    ppermute x1, waiting for transfers between devices, extended(): before = lax.ppermute(last, axis, up)  165 us
    concatenate x8, local copies, waits for them, and re-layouts, on_device(): key_tile = jnp.concatenate([near_pair[0], far_pair[0]], 0)  15.1 us
    concatenate x8, local copies, waits for them, and re-layouts, on_device(): value_tile = jnp.concatenate([near_pair[1], far_pair[1]], 0)  12.4 us
    ppermute x1, starting transfers between devices, extended(): after = lax.ppermute(initial, axis, down)  8.08 us
    gather x3, local copies, waits for them, and re-layouts, on_device(): chosen = arrived.reshape(2, piece_count, FAR_ROWS, feature_width)[:, wanted]  7.18 us
    ppermute x3, starting transfers between devices, shifted(): lax.ppermute(value, axis, [(source, source + steps) for source in range(i...  7.07 us
    slice x3, local copies, waits for them, and re-layouts, on_device(): value_tile = jnp.concatenate([near_pair[1], far_pair[1]], 0)  5.89 us
    dot_general x2, matrix products, attend(): jnp.einsum('qhd,khd->hqk', query_heads, key_heads, preferred_element_type...  5.73 us
  transfers between devices with their start and end apart: 5, of which 1 were waited for; matrix products, arithmetic and copies ran while one was open for 15% of the time, Pallas kernels for 0%

commit v1 on v0

v1 whole, which is shorter than its diff:
```python
import functools
import math

import jax
import jax.numpy as jnp
from jax import lax
from jax.experimental import pallas as pl
from jax.experimental.pallas import tpu as pltpu
from jax.sharding import PartitionSpec as P

HD = 128
FAR_ROWS = 64
FAR_SHIFTS = (2, -4, 8)
CYCLES = len(FAR_SHIFTS)
CHUNK = 512
PARTNERS = (8, -8, 4, -4, 2, -2, 1, -1)


def kernel(
    n, q_ref, k_ref, v_ref, pick_ref, o_ref, ext, stage, pick_in, pick_sm,
    near_send, near_recv, far_send, far_recv, pick_send, pick_recv, local_sem,
):
    me = lax.axis_index("tm")
    rows, width = q_ref.shape
    tile = rows // 2
    chunks = width // CHUNK
    heads = CHUNK // HD

    def present(other):
        return (other >= 0) & (other < n)

    for t, step in ((0, -1), (1, 1)):

        @pl.when(jnp.logical_not(present(me + step)))
        def _():
            for j in range(chunks):
                for kv in range(2):
                    ext[j, 2 * kv + t, :tile, :] = jnp.zeros((tile, CHUNK), ext.dtype)

    for c, shift in enumerate(FAR_SHIFTS):

        @pl.when(jnp.logical_not(present(me - shift)))
        def _():
            start = tile + c * FAR_ROWS
            for j in range(chunks):
                ext[j, :, start : start + FAR_ROWS, :] = jnp.zeros((4, FAR_ROWS, CHUNK), ext.dtype)

    barrier = pltpu.get_barrier_semaphore()
    count = jnp.int32(0)
    for step in PARTNERS:
        other = me + step
        ok = present(other)
        count = count + ok.astype(jnp.int32)

        @pl.when(ok)
        def _():
            pl.semaphore_signal(
                barrier, inc=1, device_id={"tm": other}, device_id_type=pl.DeviceIdType.MESH
            )

    pl.semaphore_wait(barrier, count)

    def pick_copy(c):
        return pltpu.make_async_remote_copy(
            src_ref=pick_ref, dst_ref=pick_in.at[c],
            send_sem=pick_send.at[c], recv_sem=pick_recv.at[c],
            device_id={"tm": me - FAR_SHIFTS[c]}, device_id_type=pl.DeviceIdType.MESH,
        )

    def near_copy(side, kv, j):
        source = (k_ref, v_ref)[kv]
        first = tile if side == 0 else 0
        return pltpu.make_async_remote_copy(
            src_ref=source.at[pl.ds(first, tile), pl.ds(pl.multiple_of(j * CHUNK, CHUNK), CHUNK)],
            dst_ref=ext.at[j, 2 * kv + side, pl.ds(0, tile), :],
            send_sem=near_send.at[2 * side + kv, j], recv_sem=near_recv.at[2 * side + kv, j],
            device_id={"tm": me + (1 - 2 * side)}, device_id_type=pl.DeviceIdType.MESH,
        )

    def far_copy(c, j):
        return pltpu.make_async_remote_copy(
            src_ref=stage.at[c, j],
            dst_ref=ext.at[j, :, pl.ds(tile + c * FAR_ROWS, FAR_ROWS), :],
            send_sem=far_send.at[c, j], recv_sem=far_recv.at[c, j],
            device_id={"tm": me + FAR_SHIFTS[c]}, device_id_type=pl.DeviceIdType.MESH,
        )

    for c in range(CYCLES):

        @pl.when(present(me - FAR_SHIFTS[c]))
        def _():
            pick_copy(c).start()

    for side in range(2):

        @pl.when(present(me + (1 - 2 * side)))
        def _():
            @pl.loop(0, chunks)
            def _(j):
                near_copy(side, 0, j).start()
                near_copy(side, 1, j).start()

    for c in range(CYCLES):

        @pl.when(present(me + FAR_SHIFTS[c]))
        def _():
            pick_copy(c).wait_recv()
            local = pltpu.make_async_copy(pick_in.at[c], pick_sm.at[c], local_sem.at[c])
            local.start()
            local.wait()

    @pl.loop(0, chunks)
    def _(j):
        columns = pl.ds(pl.multiple_of(j * CHUNK, CHUNK), CHUNK)
        for c in (2, 0, 1):

            @pl.when(present(me + FAR_SHIFTS[c]))
            def _():
                for t in range(2):
                    pick = pick_sm[c, 0, t * CYCLES + c]
                    for kv, source in enumerate((k_ref, v_ref)):
                        parts = [
                            source[p * FAR_ROWS : (p + 1) * FAR_ROWS, columns]
                            for p in range(rows // FAR_ROWS)
                        ]
                        chosen = parts[0]
                        for p in range(1, len(parts)):
                            chosen = jnp.where(pick == p, parts[p], chosen)
                        stage[c, j, 2 * kv + t] = chosen
                far_copy(c, j).start()

    scale = (1.0 / math.sqrt(HD)) * math.log2(math.e)
    extra = tile + CYCLES * FAR_ROWS
    place = lax.broadcasted_iota(jnp.int32, (1, extra), 1)
    biases = []
    for t in range(2):
        bias = jnp.where(present(me + (2 * t - 1)), 0.0, -jnp.inf)
        bias = jnp.full((1, extra), bias, jnp.float32)
        for c, shift in enumerate(FAR_SHIFTS):
            inside = place >= tile + c * FAR_ROWS
            bias = jnp.where(inside, jnp.where(present(me - shift), 0.0, -jnp.inf), bias)
        biases.append(bias)

    @pl.loop(0, chunks)
    def _(j):
        for side in range(2):

            @pl.when(present(me - (1 - 2 * side)))
            def _():
                near_copy(side, 0, j).wait_recv()
                near_copy(side, 1, j).wait_recv()

        for c in range(CYCLES):

            @pl.when(present(me - FAR_SHIFTS[c]))
            def _():
                far_copy(c, j).wait_recv()

        @pl.loop(0, heads)
        def _(i):
            columns = pl.ds(pl.multiple_of(j * CHUNK + i * HD, HD), HD)
            inner = pl.ds(pl.multiple_of(i * HD, HD), HD)
            own_keys = k_ref[:, columns]
            own_values = v_ref[:, columns]
            for t in range(2):
                query = q_ref[t * tile : (t + 1) * tile, columns]
                contract = (((1,), (1,)), ((), ()))
                own = lax.dot_general(query, own_keys, contract, preferred_element_type=jnp.float32)
                other = lax.dot_general(
                    query, ext[j, t, :, inner], contract, preferred_element_type=jnp.float32
                )
                other = other + biases[t]
                top = jnp.maximum(
                    jnp.max(own, axis=1, keepdims=True), jnp.max(other, axis=1, keepdims=True)
                )
                own = jnp.exp2((own - top) * scale)
                other = jnp.exp2((other - top) * scale)
                total = jnp.sum(own, axis=1, keepdims=True) + jnp.sum(other, axis=1, keepdims=True)
                mixed = jnp.dot(
                    own.astype(jnp.bfloat16), own_values, preferred_element_type=jnp.float32
                ) + jnp.dot(
                    other.astype(jnp.bfloat16), ext[j, 2 + t, :, inner],
                    preferred_element_type=jnp.float32,
                )
                o_ref[t * tile : (t + 1) * tile, columns] = (mixed / total).astype(o_ref.dtype)

    for c in range(CYCLES):

        @pl.when(present(me - FAR_SHIFTS[c]))
        def _():
            pick_copy(c).wait_send()

        @pl.when(present(me + FAR_SHIFTS[c]))
        def _():
            @pl.loop(0, chunks)
            def _(j):
                far_copy(c, j).wait_send()

    for side in range(2):

        @pl.when(present(me + (1 - 2 * side)))
        def _():
            @pl.loop(0, chunks)
            def _(j):
                near_copy(side, 0, j).wait_send()
                near_copy(side, 1, j).wait_send()


def on_device(queries, keys, values, far_pick):
    rows, width = queries.shape
    tiles = far_pick.shape[0]
    tile = rows // tiles
    chunks = width // CHUNK
    picks = jnp.pad(far_pick.reshape(1, -1), ((0, 7), (0, 128 - far_pick.size)))
    vmem = pl.BlockSpec(memory_space=pltpu.VMEM)
    dma = pltpu.SemaphoreType.DMA
    return pl.pallas_call(
        functools.partial(kernel, lax.axis_size("tm")),
        out_shape=jax.ShapeDtypeStruct((rows, width), queries.dtype),
        in_specs=[vmem] * 4,
        out_specs=vmem,
        scratch_shapes=[
            pltpu.VMEM((chunks, 2 * tiles, tile + CYCLES * FAR_ROWS, CHUNK), keys.dtype),
            pltpu.VMEM((CYCLES, chunks, 2 * tiles, FAR_ROWS, CHUNK), keys.dtype),
            pltpu.VMEM((CYCLES, 8, 128), jnp.int32),
            pltpu.SMEM((CYCLES, 8, 128), jnp.int32),
            dma((4, chunks)),
            dma((4, chunks)),
            dma((CYCLES, chunks)),
            dma((CYCLES, chunks)),
            dma((CYCLES,)),
            dma((CYCLES,)),
            dma((CYCLES,)),
        ],
        compiler_params=pltpu.CompilerParams(
            collective_id=0, has_side_effects=True, vmem_limit_bytes=48 * 2**20
        ),
    )(queries, keys, values, picks)


def solution(mesh):
    return jax.shard_map(
        on_device,
        mesh=mesh,
        in_specs=(
            P(("seed", "tm"), None),
            P(("seed", "tm"), None),
            P(("seed", "tm"), None),
            P("tm", None),
        ),
        out_specs=P(("seed", "tm"), None),
        check_vma=False,
    )
```

time: 255 us -> 113 us (0.44)
  the two profiles are of different devices: /device:TPU:16 before, /device:TPU:17 now
where the time goes in v1:
time: 113 us
  Pallas kernels  107 us (95%)
  local copies, waits for them, and re-layouts  5.77 us (5%)
    pallas_call x1, Pallas kernels, on_device(): pl.pallas_call(functools.partial(kernel, lax.axis_size('tm')), out_shape=...  107 us
    unnamed x7, local copies, waits for them, and re-layouts  5.01 us

profile of v1, /device:TPU:17, one launch (start us, length us, event | category | flops | bytes accessed | tf_op | source)
XLA Modules:
  0.0 112.7 jit_solution(14515246829789294314)
XLA Ops:
  0.0 0.8 reshape.3
  0.8 0.0 copy-start
  0.8 1.3 %copy-done = bf16[256,2560]{1,0:T(8,128)(2,1)S(1)} copy-done((bf16[256,2560]{1,0:T(8,128)(2,1)S(1)}, bf16[256,2560]{1,0:T(8,128)(2,1)}, u32[]{:S(2)}) %copy-start) | copy-done | bytes 1310744
  2.1 0.0 copy-start.1
  2.1 1.3 %copy-done.1 = bf16[256,2560]{1,0:T(8,128)(2,1)S(1)} copy-done((bf16[256,2560]{1,0:T(8,128)(2,1)S(1)}, bf16[256,2560]{1,0:T(8,128)(2,1)}, u32[]{:S(2)}) %copy-start.1) | copy-done | bytes 1310744
  3.4 0.0 copy-start.2
  3.4 1.3 %copy-done.2 = bf16[256,2560]{1,0:T(8,128)(2,1)S(1)} copy-done((bf16[256,2560]{1,0:T(8,128)(2,1)S(1)}, bf16[256,2560]{1,0:T(8,128)(2,1)}, u32[]{:S(2)}) %copy-start.2) | copy-done | bytes 1310744
  4.7 107.0 %shard_map.46 = bf16[256,2560]{1,0:T(8,128)(2,1)S(1)} custom-call(bf16[256,2560]{1,0:T(8,128)(2,1)S(1)} %copy-done, bf16[256,2560]{1,0:T(8,128)(2,1)S(1)} %copy-done.1, bf16[256,2560]{1,0:T(8,128)(2,1)S(1)} %copy-done.2, s32[8,128]{1,0:T(8,128)S(1)} %pad.4.pick_ref), custom_call_target="tpu_custom_call" | custom-call | tf_op jit(solution)/shard_map/pallas_call | solution.py:217
  111.7 1.1 copy.6
  (1 shorter events, 0.0 us)
Async XLA Ops:
  0.8 1.3 %copy-start = (bf16[256,2560]{1,0:T(8,128)(2,1)S(1)}, bf16[256,2560]{1,0:T(8,128)(2,1)}, u32[]{:S(2)}) copy-start(bf16[256,2560]{1,0:T(8,128)(2,1)} %q_ref.1) | copy-start | bytes 3932164
  2.1 1.3 %copy-start.1 = (bf16[256,2560]{1,0:T(8,128)(2,1)S(1)}, bf16[256,2560]{1,0:T(8,128)(2,1)}, u32[]{:S(2)}) copy-start(bf16[256,2560]{1,0:T(8,128)(2,1)} %k_ref.1) | copy-start | bytes 3932164
  3.4 1.3 %copy-start.2 = (bf16[256,2560]{1,0:T(8,128)(2,1)S(1)}, bf16[256,2560]{1,0:T(8,128)(2,1)}, u32[]{:S(2)}) copy-start(bf16[256,2560]{1,0:T(8,128)(2,1)} %v_ref.1) | copy-start | bytes 3932164

commit v2 on v1

--- a/solution.py
+++ b/solution.py
@@ -17,11 +17,18 @@
 
 
 def kernel(
-    n, q_ref, k_ref, v_ref, pick_ref, o_ref, ext, stage, pick_in, pick_sm,
-    near_send, near_recv, far_send, far_recv, pick_send, pick_recv, local_sem,
+    n, q_hbm, k_hbm, v_hbm, pick_ref, o_ref, q_ref, k_ref, v_ref, ext, stage, far_relay, near_relay,
+    pick_in, pick_sm, near_send, near_recv, far_send, far_recv, hop_recv, on_send,
+    pick_send, pick_recv, local_sem, load_sem,
 ):
     me = lax.axis_index("tm")
     rows, width = q_ref.shape
+    loads = [
+        pltpu.make_async_copy(source, target, load_sem.at[i])
+        for i, (source, target) in enumerate(((k_hbm, k_ref), (v_hbm, v_ref), (q_hbm, q_ref)))
+    ]
+    for load in loads:
+        load.start()
     tile = rows // 2
     chunks = width // CHUNK
     heads = CHUNK // HD
@@ -29,6 +36,12 @@
     def present(other):
         return (other >= 0) & (other < n)
 
+    place4 = lax.rem(me, 4)
+    far_hops = (place4 >= 2) & present(me + 2)
+    far_relays = (place4 < 2) & present(me + 4)
+    near_hops = (place4 == 3) & present(me + 1)
+    near_relays = (place4 == 1) & present(me + 3)
+
     for t, step in ((0, -1), (1, 1)):
 
         @pl.when(jnp.logical_not(present(me + step)))
@@ -47,9 +60,10 @@
 
     barrier = pltpu.get_barrier_semaphore()
     count = jnp.int32(0)
-    for step in PARTNERS:
+    greet = [(step, present(me + step)) for step in PARTNERS]
+    greet += [(3, near_relays), (-3, (place4 == 0) & present(me - 3))]
+    for step, ok in greet:
         other = me + step
-        ok = present(other)
         count = count + ok.astype(jnp.int32)
 
         @pl.when(ok)
@@ -67,23 +81,40 @@
             device_id={"tm": me - FAR_SHIFTS[c]}, device_id_type=pl.DeviceIdType.MESH,
         )
 
-    def near_copy(side, kv, j):
-        source = (k_ref, v_ref)[kv]
+    def remote(source, target, send_sem, recv_sem, step):
+        return pltpu.make_async_remote_copy(
+            src_ref=source, dst_ref=target, send_sem=send_sem, recv_sem=recv_sem,
+            device_id={"tm": me + step}, device_id_type=pl.DeviceIdType.MESH,
+        )
+
+    def near_copy(side, kv, j, hop=False):
+        source = (k_hbm, v_hbm)[kv]
         first = tile if side == 0 else 0
-        return pltpu.make_async_remote_copy(
-            src_ref=source.at[pl.ds(first, tile), pl.ds(pl.multiple_of(j * CHUNK, CHUNK), CHUNK)],
-            dst_ref=ext.at[j, 2 * kv + side, pl.ds(0, tile), :],
-            send_sem=near_send.at[2 * side + kv, j], recv_sem=near_recv.at[2 * side + kv, j],
-            device_id={"tm": me + (1 - 2 * side)}, device_id_type=pl.DeviceIdType.MESH,
+        columns = pl.ds(pl.multiple_of(j * CHUNK, CHUNK), CHUNK)
+        source = source.at[pl.ds(first, tile), columns]
+        index = 2 * side + kv
+        if hop:
+            return remote(source, near_relay.at[j], near_send.at[index, j], hop_recv.at[1, j], -2)
+        target = ext.at[j, 2 * kv + side, pl.ds(0, tile), :]
+        return remote(
+            source, target, near_send.at[index, j], near_recv.at[index, j], 1 - 2 * side
         )
 
-    def far_copy(c, j):
-        return pltpu.make_async_remote_copy(
-            src_ref=stage.at[c, j],
-            dst_ref=ext.at[j, :, pl.ds(tile + c * FAR_ROWS, FAR_ROWS), :],
-            send_sem=far_send.at[c, j], recv_sem=far_recv.at[c, j],
-            device_id={"tm": me + FAR_SHIFTS[c]}, device_id_type=pl.DeviceIdType.MESH,
-        )
+    def far_copy(c, j, hop=False):
+        cycle, (first, count) = c % 3, {0: (0, 2), 3: (2, 2)}.get(c, (0, 4))
+        source = stage.at[cycle, j, pl.ds(first, count)]
+        if hop:
+            return remote(source, far_relay.at[j], far_send.at[c, j], hop_recv.at[0, j], -2)
+        target = ext.at[j, pl.ds(first, count), pl.ds(tile + cycle * FAR_ROWS, FAR_ROWS), :]
+        return remote(source, target, far_send.at[c, j], far_recv.at[c, j], FAR_SHIFTS[cycle])
+
+    def far_on(j):
+        target = ext.at[j, pl.ds(2, 2), pl.ds(tile, FAR_ROWS), :]
+        return remote(far_relay.at[j], target, on_send.at[0, j], far_recv.at[3, j], 4)
+
+    def near_on(j):
+        target = ext.at[j, 2, pl.ds(0, tile), :]
+        return remote(near_relay.at[j], target, on_send.at[1, j], near_recv.at[1, j], 3)
 
     for c in range(CYCLES):
 
@@ -97,8 +128,19 @@
         def _():
             @pl.loop(0, chunks)
             def _(j):
+                if side == 0:
+
+                    @pl.when(near_hops)
+                    def _():
+                        near_copy(0, 1, j, hop=True).start()
+
+                    @pl.when(jnp.logical_not(near_hops))
+                    def _():
+                        near_copy(0, 1, j).start()
+
+                else:
+                    near_copy(1, 1, j).start()
                 near_copy(side, 0, j).start()
-                near_copy(side, 1, j).start()
 
     for c in range(CYCLES):
 
@@ -109,10 +151,13 @@
             local.start()
             local.wait()
 
+    loads[0].wait()
+    loads[1].wait()
+
     @pl.loop(0, chunks)
     def _(j):
         columns = pl.ds(pl.multiple_of(j * CHUNK, CHUNK), CHUNK)
-        for c in (2, 0, 1):
+        for c in (0, 2, 1):
 
             @pl.when(present(me + FAR_SHIFTS[c]))
             def _():
@@ -127,8 +172,33 @@
                         for p in range(1, len(parts)):
                             chosen = jnp.where(pick == p, parts[p], chosen)
                         stage[c, j, 2 * kv + t] = chosen
+                if c == 0:
+
+                    @pl.when(far_hops)
+                    def _():
+                        far_copy(3, j, hop=True).start()
+
+                    @pl.when(jnp.logical_not(far_hops))
+                    def _():
+                        far_copy(3, j).start()
+
                 far_copy(c, j).start()
 
+    @pl.when(near_relays)
+    def _():
+        @pl.loop(0, chunks)
+        def _(j):
+            near_copy(0, 1, j, hop=True).wait_recv()
+            near_on(j).start()
+
+    @pl.when(far_relays)
+    def _():
+        @pl.loop(0, chunks)
+        def _(j):
+            far_copy(3, j, hop=True).wait_recv()
+            far_on(j).start()
+
+    loads[2].wait()
     scale = (1.0 / math.sqrt(HD)) * math.log2(math.e)
     extra = tile + CYCLES * FAR_ROWS
     place = lax.broadcasted_iota(jnp.int32, (1, extra), 1)
@@ -155,6 +225,8 @@
             @pl.when(present(me - FAR_SHIFTS[c]))
             def _():
                 far_copy(c, j).wait_recv()
+                if c == 0:
+                    far_copy(3, j).wait_recv()
 
         @pl.loop(0, heads)
         def _(i):
@@ -195,6 +267,8 @@
             @pl.loop(0, chunks)
             def _(j):
                 far_copy(c, j).wait_send()
+                if c == 0:
+                    far_copy(3, j).wait_send()
 
     for side in range(2):
 
@@ -204,6 +278,18 @@
             def _(j):
                 near_copy(side, 0, j).wait_send()
                 near_copy(side, 1, j).wait_send()
+
+    @pl.when(near_relays)
+    def _():
+        @pl.loop(0, chunks)
+        def _(j):
+            near_on(j).wait_send()
+
+    @pl.when(far_relays)
+    def _():
+        @pl.loop(0, chunks)
+        def _(j):
+            far_on(j).wait_send()
 
 
 def on_device(queries, keys, values, far_pick):
@@ -213,27 +299,36 @@
     chunks = width // CHUNK
     picks = jnp.pad(far_pick.reshape(1, -1), ((0, 7), (0, 128 - far_pick.size)))
     vmem = pl.BlockSpec(memory_space=pltpu.VMEM)
+    hbm = pl.BlockSpec(memory_space=pl.ANY)
     dma = pltpu.SemaphoreType.DMA
     return pl.pallas_call(
         functools.partial(kernel, lax.axis_size("tm")),
         out_shape=jax.ShapeDtypeStruct((rows, width), queries.dtype),
-        in_specs=[vmem] * 4,
+        in_specs=[hbm] * 3 + [vmem],
         out_specs=vmem,
         scratch_shapes=[
+            pltpu.VMEM((rows, width), queries.dtype),
+            pltpu.VMEM((rows, width), keys.dtype),
+            pltpu.VMEM((rows, width), values.dtype),
             pltpu.VMEM((chunks, 2 * tiles, tile + CYCLES * FAR_ROWS, CHUNK), keys.dtype),
             pltpu.VMEM((CYCLES, chunks, 2 * tiles, FAR_ROWS, CHUNK), keys.dtype),
+            pltpu.VMEM((chunks, tiles, FAR_ROWS, CHUNK), values.dtype),
+            pltpu.VMEM((chunks, tile, CHUNK), values.dtype),
             pltpu.VMEM((CYCLES, 8, 128), jnp.int32),
             pltpu.SMEM((CYCLES, 8, 128), jnp.int32),
             dma((4, chunks)),
             dma((4, chunks)),
-            dma((CYCLES, chunks)),
-            dma((CYCLES, chunks)),
+            dma((CYCLES + 1, chunks)),
+            dma((CYCLES + 1, chunks)),
+            dma((2, chunks)),
+            dma((2, chunks)),
             dma((CYCLES,)),
             dma((CYCLES,)),
             dma((CYCLES,)),
+            dma((3,)),
         ],
         compiler_params=pltpu.CompilerParams(
-            collective_id=0, has_side_effects=True, vmem_limit_bytes=48 * 2**20
+            collective_id=0, has_side_effects=True, vmem_limit_bytes=56 * 2**20
         ),
     )(queries, keys, values, picks)
 

time: 113 us -> 101 us (0.89)
  Pallas kernels: 107 us -> 97.4 us
  local copies, waits for them, and re-layouts: 5.77 us -> 3.81 us
    pallas_call x1, Pallas kernels: 107 us -> 97.4 us  [on_device(): pl.pallas_call(functools.partial(kernel, lax.axis_size('tm')), out_shape=...]
    unnamed x7 -> x1, local copies, waits for them, and re-layouts: 5.01 us -> 2.46 us
where the time goes in v2:
time: 101 us
  Pallas kernels  97.4 us (96%)
  local copies, waits for them, and re-layouts  3.81 us (4%)
    pallas_call x1, Pallas kernels, on_device(): pl.pallas_call(functools.partial(kernel, lax.axis_size('tm')), out_shape=...  97.4 us
    unnamed x1, local copies, waits for them, and re-layouts  2.46 us

profile of v2, /device:TPU:17, one launch (start us, length us, event | category | flops | bytes accessed | tf_op | source)
XLA Modules:
  0.0 101.3 jit_solution(3646356755958692554)
XLA Ops:
  0.0 0.8 reshape.3
  0.8 0.6 pad.4.pick_ref
  1.4 97.4 %shard_map.46 = bf16[256,2560]{1,0:T(8,128)(2,1)} custom-call(bf16[256,2560]{1,0:T(8,128)(2,1)} %q_hbm.1, bf16[256,2560]{1,0:T(8,128)(2,1)} %k_hbm.1, bf16[256,2560]{1,0:T(8,128)(2,1)} %v_hbm.1, s32[8,128]{1,0:T(8,128)} %pad.4.pick_ref), custom_call_target="tpu_custom_call" | custom-call | tf_op jit(solution)/shard_map/pallas_call | solution.py:304
  98.8 2.5 %copy.6 = bf16[256,2560]{1,0:T(8,128)(2,1)} copy(bf16[256,2560]{1,0:T(8,128)(2,1)} %shard_map.46) | data formatting | bytes 2621440

commit v3 on v2

--- a/solution.py
+++ b/solution.py
@@ -122,25 +122,36 @@
         def _():
             pick_copy(c).start()
 
-    for side in range(2):
-
-        @pl.when(present(me + (1 - 2 * side)))
-        def _():
-            @pl.loop(0, chunks)
-            def _(j):
-                if side == 0:
-
-                    @pl.when(near_hops)
-                    def _():
-                        near_copy(0, 1, j, hop=True).start()
-
-                    @pl.when(jnp.logical_not(near_hops))
-                    def _():
-                        near_copy(0, 1, j).start()
-
-                else:
-                    near_copy(1, 1, j).start()
-                near_copy(side, 0, j).start()
+    def send_near(j):
+        @pl.when(present(me + 1))
+        def _():
+            near_copy(0, 0, j).start()
+
+            @pl.when(jnp.logical_not(near_hops))
+            def _():
+                near_copy(0, 1, j).start()
+
+        @pl.when(present(me - 1))
+        def _():
+            near_copy(1, 0, j).start()
+            near_copy(1, 1, j).start()
+
+    def fill(c, j):
+        columns = pl.ds(pl.multiple_of(j * CHUNK, CHUNK), CHUNK)
+        for t in range(2):
+            pick = pick_sm[c, 0, t * CYCLES + c]
+            for kv, source in enumerate((k_ref, v_ref)):
+                chosen = source[:FAR_ROWS, columns]
+                for p in range(1, rows // FAR_ROWS):
+                    part = source[p * FAR_ROWS : (p + 1) * FAR_ROWS, columns]
+                    chosen = jnp.where(pick == p, part, chosen)
+                stage[c, j, 2 * kv + t] = chosen
+
+    def send_far(c, j):
+        @pl.when(present(me + FAR_SHIFTS[c]))
+        def _():
+            fill(c, j)
+            far_copy(c, j).start()
 
     for c in range(CYCLES):
 
@@ -153,50 +164,55 @@
 
     loads[0].wait()
     loads[1].wait()
-
-    @pl.loop(0, chunks)
-    def _(j):
-        columns = pl.ds(pl.multiple_of(j * CHUNK, CHUNK), CHUNK)
-        for c in (0, 2, 1):
-
-            @pl.when(present(me + FAR_SHIFTS[c]))
-            def _():
-                for t in range(2):
-                    pick = pick_sm[c, 0, t * CYCLES + c]
-                    for kv, source in enumerate((k_ref, v_ref)):
-                        parts = [
-                            source[p * FAR_ROWS : (p + 1) * FAR_ROWS, columns]
-                            for p in range(rows // FAR_ROWS)
-                        ]
-                        chosen = parts[0]
-                        for p in range(1, len(parts)):
-                            chosen = jnp.where(pick == p, parts[p], chosen)
-                        stage[c, j, 2 * kv + t] = chosen
-                if c == 0:
-
-                    @pl.when(far_hops)
-                    def _():
-                        far_copy(3, j, hop=True).start()
-
-                    @pl.when(jnp.logical_not(far_hops))
-                    def _():
-                        far_copy(3, j).start()
-
-                far_copy(c, j).start()
-
-    @pl.when(near_relays)
+    send_far(2, 0)
+
+    @pl.when(present(me + 2))
     def _():
         @pl.loop(0, chunks)
         def _(j):
-            near_copy(0, 1, j, hop=True).wait_recv()
-            near_on(j).start()
-
-    @pl.when(far_relays)
+            fill(0, j)
+
+            @pl.when(far_hops)
+            def _():
+                far_copy(3, j, hop=True).start()
+
+            @pl.when(near_hops)
+            def _():
+                near_copy(0, 1, j, hop=True).start()
+
+    @pl.when(near_hops & jnp.logical_not(present(me + 2)))
     def _():
         @pl.loop(0, chunks)
         def _(j):
+            near_copy(0, 1, j, hop=True).start()
+
+    @pl.loop(0, chunks)
+    def _(j):
+        @pl.when(j + 1 < chunks)
+        def _():
+            send_far(2, j + 1)
+
+        @pl.when(present(me + 2))
+        def _():
+            far_copy(0, j).start()
+
+            @pl.when(jnp.logical_not(far_hops))
+            def _():
+                far_copy(3, j).start()
+
+        send_far(1, j)
+
+        @pl.when(far_relays)
+        def _():
             far_copy(3, j, hop=True).wait_recv()
             far_on(j).start()
+
+        @pl.when(near_relays)
+        def _():
+            near_copy(0, 1, j, hop=True).wait_recv()
+            near_on(j).start()
+
+        send_near(j)
 
     loads[2].wait()
     scale = (1.0 / math.sqrt(HD)) * math.log2(math.e)

time: 101 us -> 95.7 us (0.948); the launches traced: 101 us -> 94.1 us
  Pallas kernels: 97.4 us -> 90.3 us
    pallas_call x1, Pallas kernels: 97.4 us -> 90.3 us  [on_device(): pl.pallas_call(functools.partial(kernel, lax.axis_size('tm')), out_shape=...]
where the time goes in v3:
time: 95.7 us; the launch traced here: 94.1 us
  Pallas kernels  90.3 us (94%)
  local copies, waits for them, and re-layouts  3.81 us (4%)
    pallas_call x1, Pallas kernels, on_device(): pl.pallas_call(functools.partial(kernel, lax.axis_size('tm')), out_shape=...  90.3 us
    unnamed x1, local copies, waits for them, and re-layouts  2.46 us

profile of v3, /device:TPU:17, one launch (start us, length us, event | category | flops | bytes accessed | tf_op | source)
XLA Modules:
  0.0 94.1 jit_solution(5264313179097135162)
XLA Ops:
  0.0 0.8 reshape.3
  0.8 0.6 pad.4.pick_ref
  1.4 90.3 %shard_map.46 = bf16[256,2560]{1,0:T(8,128)(2,1)} custom-call(bf16[256,2560]{1,0:T(8,128)(2,1)} %q_hbm.1, bf16[256,2560]{1,0:T(8,128)(2,1)} %k_hbm.1, bf16[256,2560]{1,0:T(8,128)(2,1)} %v_hbm.1, s32[8,128]{1,0:T(8,128)} %pad.4.pick_ref), custom_call_target="tpu_custom_call" | custom-call | tf_op jit(solution)/shard_map/pallas_call | solution.py:320
  91.6 2.5 %copy.6 = bf16[256,2560]{1,0:T(8,128)(2,1)} copy(bf16[256,2560]{1,0:T(8,128)(2,1)} %shard_map.46) | data formatting | bytes 2621440

commit v4 on v3

--- a/solution.py
+++ b/solution.py
@@ -12,7 +12,8 @@
 FAR_ROWS = 64
 FAR_SHIFTS = (2, -4, 8)
 CYCLES = len(FAR_SHIFTS)
-CHUNK = 512
+CHUNK = 256
+AHEAD = 2
 PARTNERS = (8, -8, 4, -4, 2, -2, 1, -1)
 
 
@@ -123,13 +124,10 @@
             pick_copy(c).start()
 
     def send_near(j):
-        @pl.when(present(me + 1))
+        @pl.when(present(me + 1) & (place4 != 3))
         def _():
             near_copy(0, 0, j).start()
-
-            @pl.when(jnp.logical_not(near_hops))
-            def _():
-                near_copy(0, 1, j).start()
+            near_copy(0, 1, j).start()
 
         @pl.when(present(me - 1))
         def _():
@@ -153,6 +151,13 @@
             fill(c, j)
             far_copy(c, j).start()
 
+    @pl.when(near_hops)
+    def _():
+        @pl.loop(0, chunks)
+        def _(j):
+            near_copy(0, 1, j, hop=True).start()
+            near_copy(0, 0, j).start()
+
     for c in range(CYCLES):
 
         @pl.when(present(me + FAR_SHIFTS[c]))
@@ -164,7 +169,8 @@
 
     loads[0].wait()
     loads[1].wait()
-    send_far(2, 0)
+    for j in range(AHEAD):
+        send_far(2, j)
 
     @pl.when(present(me + 2))
     def _():
@@ -176,21 +182,21 @@
             def _():
                 far_copy(3, j, hop=True).start()
 
-            @pl.when(near_hops)
-            def _():
-                near_copy(0, 1, j, hop=True).start()
-
-    @pl.when(near_hops & jnp.logical_not(present(me + 2)))
-    def _():
-        @pl.loop(0, chunks)
-        def _(j):
-            near_copy(0, 1, j, hop=True).start()
-
     @pl.loop(0, chunks)
     def _(j):
-        @pl.when(j + 1 < chunks)
-        def _():
-            send_far(2, j + 1)
+        @pl.when(near_relays)
+        def _():
+            near_copy(0, 1, j, hop=True).wait_recv()
+            near_on(j).start()
+
+        @pl.when(far_relays)
+        def _():
+            far_copy(3, j, hop=True).wait_recv()
+            far_on(j).start()
+
+        @pl.when(j + AHEAD < chunks)
+        def _():
+            send_far(2, j + AHEAD)
 
         @pl.when(present(me + 2))
         def _():
@@ -201,17 +207,6 @@
                 far_copy(3, j).start()
 
         send_far(1, j)
-
-        @pl.when(far_relays)
-        def _():
-            far_copy(3, j, hop=True).wait_recv()
-            far_on(j).start()
-
-        @pl.when(near_relays)
-        def _():
-            near_copy(0, 1, j, hop=True).wait_recv()
-            near_on(j).start()
-
         send_near(j)
 
     loads[2].wait()
@@ -315,7 +310,7 @@
     chunks = width // CHUNK
     picks = jnp.pad(far_pick.reshape(1, -1), ((0, 7), (0, 128 - far_pick.size)))
     vmem = pl.BlockSpec(memory_space=pltpu.VMEM)
-    hbm = pl.BlockSpec(memory_space=pl.ANY)
+    hbm = pl.BlockSpec(memory_space=pltpu.HBM)
     dma = pltpu.SemaphoreType.DMA
     return pl.pallas_call(
         functools.partial(kernel, lax.axis_size("tm")),
@@ -344,7 +339,7 @@
             dma((3,)),
         ],
         compiler_params=pltpu.CompilerParams(
-            collective_id=0, has_side_effects=True, vmem_limit_bytes=56 * 2**20
+            collective_id=0, has_side_effects=True, vmem_limit_bytes=24 * 2**20
         ),
     )(queries, keys, values, picks)
 

time: 95.7 us -> 94.7 us (0.990); the launches traced: 94.1 us -> 94.5 us
  local copies, waits for them, and re-layouts: 3.81 us -> 5.77 us
  Pallas kernels: 90.3 us -> 88.7 us
    unnamed x1 -> x7, local copies, waits for them, and re-layouts: 2.46 us -> 5.01 us
    pallas_call x1, Pallas kernels: 90.3 us -> 88.7 us  [on_device(): pl.pallas_call(functools.partial(kernel, lax.axis_size('tm')), out_shape=...]
where the time goes in v4:
time: 94.7 us; the launch traced here: 94.5 us
  Pallas kernels  88.7 us (94%)
  local copies, waits for them, and re-layouts  5.77 us (6%)
    pallas_call x1, Pallas kernels, on_device(): pl.pallas_call(functools.partial(kernel, lax.axis_size('tm')), out_shape=...  88.7 us
    unnamed x7, local copies, waits for them, and re-layouts  5.01 us

profile of v4, /device:TPU:17, one launch (start us, length us, event | category | flops | bytes accessed | tf_op | source)
XLA Modules:
  0.0 94.5 jit_solution(3646703260232606585)
XLA Ops:
  0.0 0.8 reshape.3
  0.8 0.0 copy-start
  0.8 1.3 %copy-done = bf16[256,2560]{1,0:T(8,128)(2,1)S(1)} copy-done((bf16[256,2560]{1,0:T(8,128)(2,1)S(1)}, bf16[256,2560]{1,0:T(8,128)(2,1)}, u32[]{:S(2)}) %copy-start) | copy-done | bytes 1310744
  2.1 0.0 copy-start.1
  2.1 1.3 %copy-done.1 = bf16[256,2560]{1,0:T(8,128)(2,1)S(1)} copy-done((bf16[256,2560]{1,0:T(8,128)(2,1)S(1)}, bf16[256,2560]{1,0:T(8,128)(2,1)}, u32[]{:S(2)}) %copy-start.1) | copy-done | bytes 1310744
  3.4 0.0 copy-start.2
  3.4 1.3 %copy-done.2 = bf16[256,2560]{1,0:T(8,128)(2,1)S(1)} copy-done((bf16[256,2560]{1,0:T(8,128)(2,1)S(1)}, bf16[256,2560]{1,0:T(8,128)(2,1)}, u32[]{:S(2)}) %copy-start.2) | copy-done | bytes 1310744
  4.7 88.7 %shard_map.46 = bf16[256,2560]{1,0:T(8,128)(2,1)S(1)} custom-call(bf16[256,2560]{1,0:T(8,128)(2,1)S(1)} %copy-done, bf16[256,2560]{1,0:T(8,128)(2,1)S(1)} %copy-done.1, bf16[256,2560]{1,0:T(8,128)(2,1)S(1)} %copy-done.2, s32[8,128]{1,0:T(8,128)S(1)} %pad.4.pick_ref), custom_call_target="tpu_custom_call" | custom-call | tf_op jit(solution)/shard_map/pallas_call | solution.py:315
  93.4 1.1 %copy.6 = bf16[256,2560]{1,0:T(8,128)(2,1)} copy(bf16[256,2560]{1,0:T(8,128)(2,1)S(1)} %shard_map.46) | data formatting | bytes 2621440
  (1 shorter events, 0.0 us)
Async XLA Ops:
  0.8 1.3 %copy-start = (bf16[256,2560]{1,0:T(8,128)(2,1)S(1)}, bf16[256,2560]{1,0:T(8,128)(2,1)}, u32[]{:S(2)}) copy-start(bf16[256,2560]{1,0:T(8,128)(2,1)} %q_hbm.1) | copy-start | bytes 3932164
  2.1 1.3 %copy-start.1 = (bf16[256,2560]{1,0:T(8,128)(2,1)S(1)}, bf16[256,2560]{1,0:T(8,128)(2,1)}, u32[]{:S(2)}) copy-start(bf16[256,2560]{1,0:T(8,128)(2,1)} %k_hbm.1) | copy-start | bytes 3932164
  3.4 1.3 %copy-start.2 = (bf16[256,2560]{1,0:T(8,128)(2,1)S(1)}, bf16[256,2560]{1,0:T(8,128)(2,1)}, u32[]{:S(2)}) copy-start(bf16[256,2560]{1,0:T(8,128)(2,1)} %v_hbm.1) | copy-start | bytes 3932164

commit v5 on v4

--- a/solution.py
+++ b/solution.py
@@ -33,6 +33,7 @@
     tile = rows // 2
     chunks = width // CHUNK
     heads = CHUNK // HD
+    near_hop_chunks = chunks * 7 // 10
 
     def present(other):
         return (other >= 0) & (other < n)
@@ -155,7 +156,14 @@
     def _():
         @pl.loop(0, chunks)
         def _(j):
-            near_copy(0, 1, j, hop=True).start()
+            @pl.when(j < near_hop_chunks)
+            def _():
+                near_copy(0, 1, j, hop=True).start()
+
+            @pl.when(j >= near_hop_chunks)
+            def _():
+                near_copy(0, 1, j).start()
+
             near_copy(0, 0, j).start()
 
     for c in range(CYCLES):
@@ -184,7 +192,7 @@
 
     @pl.loop(0, chunks)
     def _(j):
-        @pl.when(near_relays)
+        @pl.when(near_relays & (j < near_hop_chunks))
         def _():
             near_copy(0, 1, j, hop=True).wait_recv()
             near_on(j).start()
@@ -292,7 +300,7 @@
 
     @pl.when(near_relays)
     def _():
-        @pl.loop(0, chunks)
+        @pl.loop(0, near_hop_chunks)
         def _(j):
             near_on(j).wait_send()
 
@@ -339,7 +347,7 @@
             dma((3,)),
         ],
         compiler_params=pltpu.CompilerParams(
-            collective_id=0, has_side_effects=True, vmem_limit_bytes=24 * 2**20
+            collective_id=0, has_side_effects=True, vmem_limit_bytes=52 * 2**20
         ),
     )(queries, keys, values, picks)
 

time: 94.7 us -> 91.8 us (0.969)
  local copies, waits for them, and re-layouts: 5.77 us -> 1.82 us
  Pallas kernels: 88.7 us -> 89.8 us
    unnamed x7 -> x1, local copies, waits for them, and re-layouts: 5.01 us -> 1.06 us
    pallas_call x1, Pallas kernels: 88.7 us -> 89.8 us  [on_device(): pl.pallas_call(functools.partial(kernel, lax.axis_size('tm')), out_shape=...]
where the time goes in v5:
time: 91.8 us; the launch traced here: 91.7 us
  Pallas kernels  89.8 us (98%)
  local copies, waits for them, and re-layouts  1.82 us (2%)
    pallas_call x1, Pallas kernels, on_device(): pl.pallas_call(functools.partial(kernel, lax.axis_size('tm')), out_shape=...  89.8 us

profile of v5, /device:TPU:17, one launch (start us, length us, event | category | flops | bytes accessed | tf_op | source)
XLA Modules:
  0.0 91.7 jit_solution(16622166344348771073)
XLA Ops:
  0.0 0.8 reshape.3
  0.8 89.8 %shard_map.46 = bf16[256,2560]{1,0:T(8,128)(2,1)S(1)} custom-call(bf16[256,2560]{1,0:T(8,128)(2,1)} %q_hbm.1, bf16[256,2560]{1,0:T(8,128)(2,1)} %k_hbm.1, bf16[256,2560]{1,0:T(8,128)(2,1)} %v_hbm.1, s32[8,128]{1,0:T(8,128)S(1)} %pad.4.pick_ref), custom_call_target="tpu_custom_call" | custom-call | tf_op jit(solution)/shard_map/pallas_call | solution.py:323
  90.6 1.1 %copy.6 = bf16[256,2560]{1,0:T(8,128)(2,1)} copy(bf16[256,2560]{1,0:T(8,128)(2,1)S(1)} %shard_map.46) | data formatting | bytes 2621440
  (1 shorter events, 0.0 us)

commit v6 on v5

--- a/solution.py
+++ b/solution.py
@@ -13,7 +13,7 @@
 FAR_SHIFTS = (2, -4, 8)
 CYCLES = len(FAR_SHIFTS)
 CHUNK = 256
-AHEAD = 2
+AHEAD = 1
 PARTNERS = (8, -8, 4, -4, 2, -2, 1, -1)
 
 
@@ -202,17 +202,17 @@
             far_copy(3, j, hop=True).wait_recv()
             far_on(j).start()
 
+        @pl.when(present(me + 2))
+        def _():
+            far_copy(0, j).start()
+
+            @pl.when(jnp.logical_not(far_hops))
+            def _():
+                far_copy(3, j).start()
+
         @pl.when(j + AHEAD < chunks)
         def _():
             send_far(2, j + AHEAD)
-
-        @pl.when(present(me + 2))
-        def _():
-            far_copy(0, j).start()
-
-            @pl.when(jnp.logical_not(far_hops))
-            def _():
-                far_copy(3, j).start()
 
         send_far(1, j)
         send_near(j)

time: 91.8 us -> 90 us (0.980)
  Pallas kernels: 89.8 us -> 88.1 us
    pallas_call x1, Pallas kernels: 89.8 us -> 88.1 us  [on_device(): pl.pallas_call(functools.partial(kernel, lax.axis_size('tm')), out_shape=...]
where the time goes in v6:
time: 90 us; the launch traced here: 89.9 us
  Pallas kernels  88.1 us (98%)
  local copies, waits for them, and re-layouts  1.82 us (2%)
    pallas_call x1, Pallas kernels, on_device(): pl.pallas_call(functools.partial(kernel, lax.axis_size('tm')), out_shape=...  88.1 us

profile of v6, /device:TPU:17, one launch (start us, length us, event | category | flops | bytes accessed | tf_op | source)
XLA Modules:
  0.0 89.9 jit_solution(5005145291434168819)
XLA Ops:
  0.0 0.8 reshape.3
  0.8 88.1 %shard_map.46 = bf16[256,2560]{1,0:T(8,128)(2,1)S(1)} custom-call(bf16[256,2560]{1,0:T(8,128)(2,1)} %q_hbm.1, bf16[256,2560]{1,0:T(8,128)(2,1)} %k_hbm.1, bf16[256,2560]{1,0:T(8,128)(2,1)} %v_hbm.1, s32[8,128]{1,0:T(8,128)S(1)} %pad.4.pick_ref), custom_call_target="tpu_custom_call" | custom-call | tf_op jit(solution)/shard_map/pallas_call | solution.py:323
  88.8 1.1 %copy.6 = bf16[256,2560]{1,0:T(8,128)(2,1)} copy(bf16[256,2560]{1,0:T(8,128)(2,1)S(1)} %shard_map.46) | data formatting | bytes 2621440
  (1 shorter events, 0.0 us)
